TPU v7x, 32 devices: a whole 2x2x4 slice. The times are simulated.
32 devices in a mesh: section: 2 (over core), replica: 4 (over z), shard: 4 (over y, x).
Axes of the slice: x: 2, y: 2, z: 4, core: 2. Of those that a mesh axis runs over, the one named last changes fastest.
Arguments:
- inputs: bfloat16 [2, 4, 1024, 1088], P(None, 'replica', 'shard'), may hold values from -6 to 6
- cotangent: bfloat16 [2, 4, 1024, 1088], P(None, 'replica', 'shard'), may hold values from -6 to 6
- segments: int32 [2, 4, 1024], P(None, 'replica'), may hold values from 0 to 3, as said below
- ln1_gain: bfloat16 [2, 1088], P('section', 'shard'), may hold values from 0.5 to 1.5
- ln1_bias: bfloat16 [2, 1088], P('section', 'shard'), may hold values from -1.5 to 1.5
- w_qkv: bfloat16 [2, 1088, 3264], P('section', 'shard'), may hold values from -0.1875 to 0.1875
- w_out: bfloat16 [2, 1088, 1088], P('section', 'shard'), may hold values from -0.75 to 0.75
- out_bias: bfloat16 [2, 1088], P('section', 'shard'), may hold values from -1.5 to 1.5
- ln2_gain: bfloat16 [2, 1088], P('section', 'shard'), may hold values from 0.5 to 1.5
- ln2_bias: bfloat16 [2, 1088], P('section', 'shard'), may hold values from -1.5 to 1.5
- w_up: bfloat16 [2, 1088, 4352], P('section', 'shard'), may hold values from -0.1875 to 0.1875
- up_bias: bfloat16 [2, 4352], P('section', 'shard'), may hold values from -1.5 to 1.5
- w_down: bfloat16 [2, 4352, 1088], P('section', 'shard'), may hold values from -0.09375 to 0.09375
- down_bias: bfloat16 [2, 1088], P('section', 'shard'), may hold values from -1.5 to 1.5
Outputs:
- section_outputs: bfloat16 [2, 2, 4, 1024, 1088], P('section', None, 'replica', 'shard')
- input_grads: bfloat16 [2, 2, 4, 1024, 1088], P('section', None, 'replica', 'shard')
- grad_ln1_gain: float32 [2, 1088], P('section', 'shard')
- grad_ln1_bias: float32 [2, 1088], P('section', 'shard')
- grad_w_qkv: float32 [2, 1088, 3264], P('section', 'shard')
- grad_w_out: float32 [2, 1088, 1088], P('section', 'shard')
- grad_out_bias: float32 [2, 1088], P('section', 'shard')
- grad_ln2_gain: float32 [2, 1088], P('section', 'shard')
- grad_ln2_bias: float32 [2, 1088], P('section', 'shard')
- grad_w_up: float32 [2, 1088, 4352], P('section', 'shard')
- grad_up_bias: float32 [2, 4352], P('section', 'shard')
- grad_w_down: float32 [2, 4352, 1088], P('section', 'shard')
- grad_down_bias: float32 [2, 1088], P('section', 'shard')
Inputs may be any that keep to these rules, and one draw needn't show every extreme that they name: `segments`: in every sequence the document number starts at 0 at the first token and never falls; of the 2 sequences that share a replica index, one is a single document and every other one holds exactly four documents.
All inputs are finite; a program needn't handle non-finite values.
Results may differ from a plain program's by a relative error of at most 0.015.
Values may be sent and summed in bfloat16 or wider, within the bound.
No kernel may reach another device: no remote copies, remote signals or barrier semaphores. Data moves between devices by JAX's collectives and lax.ppermute only.
A program may use at most 384 MiB of HBM per device.

v0:
```python
import math

import jax
import jax.numpy as jnp
from jax import lax
from jax.sharding import PartitionSpec as P

HD = 64


norm_eps = 1e-05


def from_behind(block, axis, distance):
    devices = range(lax.axis_size(axis))
    route = [(i - distance, i) for i in devices if i - distance in devices]
    return lax.ppermute(block, axis, route)


def layer_norm(values, gain, bias):
    centre = jnp.mean(values, -1, keepdims=True)
    centered = values - centre
    spread = jnp.mean(centered * centered, -1, keepdims=True)
    return centered * lax.rsqrt(spread + norm_eps) * gain + bias


def smooth_gate(values):
    return jax.nn.gelu(values, approximate=True)


def contract_rows(left, right):
    return lax.dot_general(
        left, right, (((0,), (0,)), ((), ())), preferred_element_type=jnp.float32
    )


def times_transpose(left, right):
    return lax.dot_general(
        left, right, (((1,), (1,)), ((), ())), preferred_element_type=jnp.float32
    )


def local(
    inputs,
    cotangent,
    segments,
    ln1_gain,
    ln1_bias,
    w_qkv,
    w_out,
    out_bias,
    ln2_gain,
    ln2_bias,
    w_up,
    up_bias,
    w_down,
    down_bias,
):
    params = (
        ln1_gain,
        ln1_bias,
        w_qkv,
        w_out,
        out_bias,
        ln2_gain,
        ln2_bias,
        w_up,
        up_bias,
        w_down,
        down_bias,
    )
    first = lax.axis_index("section") == 0
    shard_place = lax.axis_index("shard")
    mb_count, seq_rep, span, width = inputs.shape
    length = segments.shape[2]
    heads = width // HD
    scale = 1.0 / math.sqrt(HD)
    row_count = seq_rep * span
    gathered = (
        lax.all_gather(params[0], "shard", axis=1, tiled=True),
        lax.all_gather(params[1], "shard", axis=1, tiled=True),
        lax.all_gather(params[2], "shard", axis=1, tiled=True),
        lax.all_gather(params[3], "shard", axis=1, tiled=True),
        lax.all_gather(params[4], "shard", axis=1, tiled=True),
        lax.all_gather(params[5], "shard", axis=1, tiled=True),
        lax.all_gather(params[6], "shard", axis=1, tiled=True),
        lax.all_gather(params[7], "shard", axis=1, tiled=True),
        lax.all_gather(params[8], "shard", axis=1, tiled=True),
        lax.all_gather(params[9], "shard", axis=1, tiled=True),
        lax.all_gather(params[10], "shard", axis=1, tiled=True),
    )
    fwd_weights = tuple((piece[0] for piece in gathered))
    key_place = jnp.arange(length)
    query_place = shard_place * span + jnp.arange(span)

    def attend_scores(query_heads, key_heads, mask):
        scores = (
            jnp.einsum(
                "sqhd,skhd->shqk", query_heads, key_heads, preferred_element_type=jnp.float32
            )
            * scale
        )
        return jnp.where(mask[:, None], scores, -1e30)

    def split_project(project):
        queries = project[:, :width].reshape(seq_rep, span, width)
        keys_local = project[:, width : 2 * width].reshape(seq_rep, span, width)
        values_local = project[:, 2 * width :].reshape(seq_rep, span, width)
        return (queries, keys_local, values_local)

    received = jnp.zeros((seq_rep, span, width), jnp.bfloat16)
    outputs_slot = []
    saved_slot = []
    for slot in range(mb_count + 1):
        fresh = inputs[min(slot, mb_count - 1)]
        hidden_low = jnp.where(first, fresh, received)
        slot_segment = jnp.where(
            first, segments[min(slot, mb_count - 1)], segments[max(slot - 1, 0)]
        )
        query_seg = lax.dynamic_slice_in_dim(slot_segment, shard_place * span, span, 1)
        same_doc = query_seg[:, :, None] == slot_segment[:, None, :]
        mask = same_doc & (key_place[None, None, :] <= query_place[None, :, None])
        (
            forward_gain_one,
            forward_bias_one,
            forward_proj_qkv,
            forward_proj_out,
            forward_bias_out,
            forward_gain_two,
            forward_bias_two,
            forward_proj_up,
            forward_bias_up,
            forward_proj_down,
            forward_bias_down,
        ) = fwd_weights
        hidden = hidden_low.astype(jnp.float32).reshape(row_count, width)
        normed = layer_norm(
            hidden, forward_gain_one.astype(jnp.float32), forward_bias_one.astype(jnp.float32)
        ).astype(jnp.bfloat16)
        forward_project = jnp.dot(
            normed, forward_proj_qkv, preferred_element_type=jnp.float32
        ).astype(jnp.bfloat16)
        forward_queries, forward_keys_local, forward_values_local = split_project(forward_project)
        forward_keys_all = lax.all_gather(forward_keys_local, "shard", axis=1, tiled=True)
        forward_values_all = lax.all_gather(forward_values_local, "shard", axis=1, tiled=True)
        forward_query_heads = forward_queries.reshape(seq_rep, span, heads, HD)
        forward_key_heads = forward_keys_all.reshape(seq_rep, length, heads, HD)
        forward_value_heads = forward_values_all.reshape(seq_rep, length, heads, HD)
        forward_scores = attend_scores(forward_query_heads, forward_key_heads, mask)
        peak = jnp.max(forward_scores, -1, keepdims=True)
        raised = jnp.exp(forward_scores - peak)
        total = jnp.sum(raised, -1, keepdims=True)
        forward_probs = (raised / total).astype(jnp.bfloat16)
        log_total = peak + jnp.log(total)
        mixed = jnp.einsum(
            "shqk,skhd->sqhd",
            forward_probs,
            forward_value_heads,
            preferred_element_type=jnp.float32,
        )
        mixed = mixed.reshape(row_count, width).astype(jnp.bfloat16)
        middle = (
            hidden
            + jnp.dot(mixed, forward_proj_out, preferred_element_type=jnp.float32)
            + forward_bias_out.astype(jnp.float32)
        )
        normed_two = layer_norm(
            middle, forward_gain_two.astype(jnp.float32), forward_bias_two.astype(jnp.float32)
        ).astype(jnp.bfloat16)
        gate_in = jnp.dot(
            normed_two, forward_proj_up, preferred_element_type=jnp.float32
        ) + forward_bias_up.astype(jnp.float32)
        activated = smooth_gate(gate_in).astype(jnp.bfloat16)
        result = (
            middle
            + jnp.dot(activated, forward_proj_down, preferred_element_type=jnp.float32)
            + forward_bias_down.astype(jnp.float32)
        )
        forward_saved = {
            "hidden": hidden,
            "normed": normed,
            "project": forward_project,
            "log_total": log_total,
            "mixed": mixed,
            "middle": middle,
            "normed_two": normed_two,
            "gate_in": gate_in,
            "activated": activated,
            "mask": mask,
            "segment": slot_segment,
            "keys_all": forward_keys_all,
            "values_all": forward_values_all,
        }
        result, saved = (result.astype(jnp.bfloat16), forward_saved)
        outputs_slot.append(result.reshape(seq_rep, span, width))
        saved_slot.append(saved)
        if slot < mb_count:
            received = from_behind(result.reshape(seq_rep, span, width), "section", 1)
    section_outputs = jnp.stack(
        [
            jnp.where(first, outputs_slot[index], outputs_slot[index + 1])
            for index in range(mb_count)
        ]
    )[None]

    def pick_section(late_piece, early_piece):
        return jnp.where(first, early_piece, late_piece)

    returned = jnp.zeros((seq_rep, span, width), jnp.bfloat16)
    grads_slot = []
    pieces_all = []
    saved_used = []
    for slot in range(mb_count + 1):
        saved = jax.tree.map(
            pick_section, saved_slot[min(slot + 1, mb_count)], saved_slot[max(slot - 1, 0)]
        )
        fresh = cotangent[min(slot, mb_count - 1)].astype(jnp.float32)
        grad_out = jnp.where(first, returned.astype(jnp.float32), fresh).reshape(row_count, width)
        active = jnp.where(first, slot >= 1, slot < mb_count)
        grad_out = jnp.where(active, grad_out, 0.0)
        (
            gain_one,
            bias_one,
            proj_qkv,
            proj_out,
            bias_out,
            gain_two,
            bias_two,
            proj_up,
            bias_up,
            proj_down,
            bias_down,
        ) = fwd_weights
        grad_branch = grad_out.astype(jnp.bfloat16)
        grad_act = times_transpose(grad_branch, proj_down)
        grad_gate = jax.vjp(smooth_gate, saved["gate_in"])[1](grad_act)[0].astype(jnp.bfloat16)
        grad_normed_two = times_transpose(grad_gate, proj_up)
        norm_pull_two = jax.vjp(
            layer_norm, saved["middle"], gain_two.astype(jnp.float32), bias_two.astype(jnp.float32)
        )[1]
        grad_mid, grad_gain_two, grad_bias_two = norm_pull_two(grad_normed_two)
        grad_middle = grad_out + grad_mid
        grad_attn = grad_middle.astype(jnp.bfloat16)
        grad_mixed = (
            times_transpose(grad_attn, proj_out)
            .astype(jnp.bfloat16)
            .reshape(seq_rep, span, heads, HD)
        )
        backward_queries, backward_keys_local, backward_values_local = split_project(
            saved["project"]
        )
        keys_all = saved["keys_all"]
        values_all = saved["values_all"]
        backward_query_heads = backward_queries.reshape(seq_rep, span, heads, HD)
        backward_key_heads = keys_all.reshape(seq_rep, length, heads, HD)
        value_heads = values_all.reshape(seq_rep, length, heads, HD)
        backward_scores = attend_scores(backward_query_heads, backward_key_heads, saved["mask"])
        probs = jnp.exp(backward_scores - saved["log_total"])
        grad_probs = jnp.einsum(
            "sqhd,skhd->shqk", grad_mixed, value_heads, preferred_element_type=jnp.float32
        )
        inner = jnp.sum(probs * grad_probs, -1, keepdims=True)
        grad_scores = (probs * (grad_probs - inner)).astype(jnp.bfloat16)
        grad_queries = (
            jnp.einsum(
                "shqk,skhd->sqhd",
                grad_scores,
                backward_key_heads,
                preferred_element_type=jnp.float32,
            )
            * scale
        )
        all_queries = lax.all_gather(backward_query_heads, "shard", axis=1, tiled=True)
        all_grad_mixed = lax.all_gather(grad_mixed, "shard", axis=1, tiled=True)
        all_log_total = lax.all_gather(saved["log_total"], "shard", axis=2, tiled=True)
        all_inner = lax.all_gather(inner, "shard", axis=2, tiled=True)
        own_keys = backward_keys_local.reshape(seq_rep, span, heads, HD)
        own_values = backward_values_local.reshape(seq_rep, span, heads, HD)
        backward_segment = saved["segment"]
        key_seg = lax.dynamic_slice_in_dim(backward_segment, shard_place * span, span, 1)
        own_place = shard_place * span + jnp.arange(span)
        mask_keys = (backward_segment[:, :, None] == key_seg[:, None, :]) & (
            own_place[None, None, :] <= key_place[None, :, None]
        )
        scores_keys = attend_scores(all_queries, own_keys, mask_keys)
        probs_keys = jnp.exp(scores_keys - all_log_total)
        grad_probs_keys = jnp.einsum(
            "sqhd,skhd->shqk", all_grad_mixed, own_values, preferred_element_type=jnp.float32
        )
        grad_scores_keys = (probs_keys * (grad_probs_keys - all_inner)).astype(jnp.bfloat16)
        grad_keys = (
            jnp.einsum(
                "shqk,sqhd->skhd", grad_scores_keys, all_queries, preferred_element_type=jnp.float32
            )
            * scale
        )
        grad_values = jnp.einsum(
            "shqk,sqhd->skhd",
            probs_keys.astype(jnp.bfloat16),
            all_grad_mixed,
            preferred_element_type=jnp.float32,
        )
        grad_project = jnp.concatenate(
            [
                grad_queries.reshape(row_count, width),
                grad_keys.reshape(row_count, width),
                grad_values.reshape(row_count, width),
            ],
            1,
        ).astype(jnp.bfloat16)
        grad_normed = times_transpose(grad_project, proj_qkv)
        norm_pull_one = jax.vjp(
            layer_norm, saved["hidden"], gain_one.astype(jnp.float32), bias_one.astype(jnp.float32)
        )[1]
        grad_hidden, grad_gain_one, grad_bias_one = norm_pull_one(grad_normed)
        grad_input = grad_middle + grad_hidden
        grad_input, pieces = (
            grad_input,
            (
                grad_branch,
                grad_gate,
                grad_attn,
                grad_project,
                grad_gain_one,
                grad_bias_one,
                grad_gain_two,
                grad_bias_two,
            ),
        )
        grad_low = grad_input.astype(jnp.bfloat16).reshape(seq_rep, span, width)
        grads_slot.append(grad_low)
        pieces_all.append(pieces)
        saved_used.append(saved)
        if slot < mb_count:
            returned = from_behind(grad_low, "section", -1)
    input_grads = jnp.stack(
        [jnp.where(first, grads_slot[index + 1], grads_slot[index]) for index in range(mb_count)]
    )[None]

    def stacked(label):
        return jnp.concatenate([entry[label] for entry in saved_used], 0)

    def grads_of(number):
        return jnp.concatenate([entry[number] for entry in pieces_all], 0)

    def summed_terms(number):
        return jnp.sum(jnp.stack([entry[number] for entry in pieces_all]), 0)

    own_width = ln1_gain.shape[1]
    own_hidden = up_bias.shape[1]
    columns = (
        lax.all_to_all(stacked("normed"), "shard", split_axis=1, concat_axis=0, tiled=True),
        lax.all_to_all(stacked("mixed"), "shard", split_axis=1, concat_axis=0, tiled=True),
        lax.all_to_all(stacked("normed_two"), "shard", split_axis=1, concat_axis=0, tiled=True),
        lax.all_to_all(stacked("activated"), "shard", split_axis=1, concat_axis=0, tiled=True),
    )
    piece_branch = lax.all_gather(grads_of(0), "shard", axis=0, tiled=True)
    piece_gate = lax.all_gather(grads_of(1), "shard", axis=0, tiled=True)
    piece_attn = lax.all_gather(grads_of(2), "shard", axis=0, tiled=True)
    piece_project = lax.all_gather(grads_of(3), "shard", axis=0, tiled=True)
    qkv_sum = contract_rows(columns[0], piece_project)
    out_sum = contract_rows(columns[1], piece_attn)
    up_sum = contract_rows(columns[2], piece_gate)
    down_sum = contract_rows(columns[3], piece_branch)
    out_bsum = jnp.sum(
        lax.dynamic_slice_in_dim(piece_attn, shard_place * own_width, own_width, 1).astype(
            jnp.float32
        ),
        0,
    )
    up_bsum = jnp.sum(
        lax.dynamic_slice_in_dim(piece_gate, shard_place * own_hidden, own_hidden, 1).astype(
            jnp.float32
        ),
        0,
    )
    down_bsum = jnp.sum(
        lax.dynamic_slice_in_dim(piece_branch, shard_place * own_width, own_width, 1).astype(
            jnp.float32
        ),
        0,
    )
    norm_shares = (
        lax.psum_scatter(summed_terms(4)[None], "shard", scatter_dimension=1, tiled=True),
        lax.psum_scatter(summed_terms(5)[None], "shard", scatter_dimension=1, tiled=True),
        lax.psum_scatter(summed_terms(6)[None], "shard", scatter_dimension=1, tiled=True),
        lax.psum_scatter(summed_terms(7)[None], "shard", scatter_dimension=1, tiled=True),
    )
    shares = (
        norm_shares[0],
        norm_shares[1],
        qkv_sum[None],
        out_sum[None],
        out_bsum[None],
        norm_shares[2],
        norm_shares[3],
        up_sum[None],
        up_bsum[None],
        down_sum[None],
        down_bsum[None],
    )
    summed = (
        lax.psum(shares[0].astype(jnp.bfloat16), "replica").astype(jnp.float32),
        lax.psum(shares[1].astype(jnp.bfloat16), "replica").astype(jnp.float32),
        lax.psum(shares[2].astype(jnp.bfloat16), "replica").astype(jnp.float32),
        lax.psum(shares[3].astype(jnp.bfloat16), "replica").astype(jnp.float32),
        lax.psum(shares[4].astype(jnp.bfloat16), "replica").astype(jnp.float32),
        lax.psum(shares[5].astype(jnp.bfloat16), "replica").astype(jnp.float32),
        lax.psum(shares[6].astype(jnp.bfloat16), "replica").astype(jnp.float32),
        lax.psum(shares[7].astype(jnp.bfloat16), "replica").astype(jnp.float32),
        lax.psum(shares[8].astype(jnp.bfloat16), "replica").astype(jnp.float32),
        lax.psum(shares[9].astype(jnp.bfloat16), "replica").astype(jnp.float32),
        lax.psum(shares[10].astype(jnp.bfloat16), "replica").astype(jnp.float32),
    )
    return (
        section_outputs,
        input_grads,
        summed[0],
        summed[1],
        summed[2],
        summed[3],
        summed[4],
        summed[5],
        summed[6],
        summed[7],
        summed[8],
        summed[9],
        summed[10],
    )


def solution(mesh):
    return jax.shard_map(
        local,
        mesh=mesh,
        in_specs=(
            P(None, "replica", "shard", None),
            P(None, "replica", "shard", None),
            P(None, "replica", None),
            P("section", "shard"),
            P("section", "shard"),
            P("section", "shard", None),
            P("section", "shard", None),
            P("section", "shard"),
            P("section", "shard"),
            P("section", "shard"),
            P("section", "shard", None),
            P("section", "shard"),
            P("section", "shard", None),
            P("section", "shard"),
        ),
        out_specs=(
            P("section", None, "replica", "shard", None),
            P("section", None, "replica", "shard", None),
            P("section", "shard"),
            P("section", "shard"),
            P("section", "shard", None),
            P("section", "shard", None),
            P("section", "shard"),
            P("section", "shard"),
            P("section", "shard"),
            P("section", "shard", None),
            P("section", "shard"),
            P("section", "shard", None),
            P("section", "shard"),
        ),
        check_vma=False,
    )
```

profile of v0, /device:TPU:0, one launch (start us, length us, event | category | flops | bytes accessed | tf_op | source)
XLA Modules:
  0.0 1942.8 jit_solution(17010926446594599000)
XLA Ops:
  17.2 19.6 %all-reduce.12 = (bf16[1088]{0:T(1024)(128)(2,1)S(1)}, bf16[1088]{0:T(1024)(128)(2,1)S(1)}, bf16[1088]{0:T(1024)(128)(2,1)S(1)}, bf16[1088]{0:T(1024)(128)(2,1)S...) all-reduce(bf16[1088]{0:T(1024)(128)(2,1)S(1)} %dynamic-update-slic, ...), channel_id=1, replica_groups=mesh['section'=2,'replica'=4,'shard'=4] {'shard'}, use_global_device_ids=true, to_apply=%add.1 | all-reduce | flops 10880 | bytes 43520
  37.3 54.2 %all-gather.33.cloned.1.call-done = bf16[1,1088,3264]{2,1,0:T(8,128)(2,1)} async-done(((bf16[1,272,3264]{2,1,0:T(8,128)(2,1)}), bf16[1,1088,3264]{2,1,0:T(8,128)(2,1)}) %all-gather.33.cloned.1.call-update) | async-done | bytes 7102480 | tf_op jit(solution)/shard_map/all_gather | solution.py:82
  105.7 31.1 %all-gather.63.cloned.1.call-done = bf16[1024,1088]{0,1:T(8,128)(2,1)} async-done(((bf16[256,1088]{0,1:T(8,128)(2,1)}), bf16[1024,1088]{0,1:T(8,128)(2,1)}) %all-gather.63.cloned.1.call-update) | async-done | bytes 2228240 | tf_op jit(solution)/shard_map/all_gather | solution.py:144
  152.9 22.6 %all-gather.61.cloned.1.call-done = bf16[1024,1088]{0,1:T(8,128)(2,1)} async-done(((bf16[256,1088]{0,1:T(8,128)(2,1)}), bf16[1024,1088]{0,1:T(8,128)(2,1)}) %all-gather.61.cloned.1.call-update) | async-done | bytes 2228240 | tf_op jit(solution)/shard_map/all_gather | solution.py:145
  185.1 30.9 %all-gather.35.cloned.1.call-done = bf16[1,1088,1088]{2,1,0:T(8,128)(2,1)} async-done(((bf16[1,272,1088]{2,1,0:T(8,128)(2,1)}), bf16[1,1088,1088]{2,1,0:T(8,128)(2,1)}) %all-gather.35.cloned.1.call-update) | async-done | bytes 2367504 | tf_op jit(solution)/shard_map/all_gather | solution.py:83
  219.1 95.2 %all-gather.37.cloned.1.call-done = bf16[1,1088,4352]{2,1,0:T(8,128)(2,1)} async-done(((bf16[1,272,4352]{2,1,0:T(8,128)(2,1)}), bf16[1,1088,4352]{2,1,0:T(8,128)(2,1)}) %all-gather.37.cloned.1.call-update) | async-done | bytes 9469968 | tf_op jit(solution)/shard_map/all_gather | solution.py:87
  323.5 93.8 %all-gather.39.cloned.1.call-done = bf16[1,4352,1088]{2,1,0:T(8,128)(2,1)} async-done(((bf16[1,1088,1088]{2,1,0:T(8,128)(2,1)}), bf16[1,4352,1088]{2,1,0:T(8,128)(2,1)}) %all-gather.39.cloned.1.call-update) | async-done | bytes 9469968 | tf_op jit(solution)/shard_map/all_gather | solution.py:89
  446.0 31.4 %all-gather.67.cloned.1.call-done = bf16[1024,1088]{0,1:T(8,128)(2,1)} async-done(((bf16[256,1088]{0,1:T(8,128)(2,1)}), bf16[1024,1088]{0,1:T(8,128)(2,1)}) %all-gather.67.cloned.1.call-update) | async-done | bytes 2228240 | tf_op jit(solution)/shard_map/all_gather | solution.py:144
  494.5 21.6 %all-gather.65.cloned.1.call-done = bf16[1024,1088]{0,1:T(8,128)(2,1)} async-done(((bf16[256,1088]{0,1:T(8,128)(2,1)}), bf16[1024,1088]{0,1:T(8,128)(2,1)}) %all-gather.65.cloned.1.call-update) | async-done | bytes 2228240 | tf_op jit(solution)/shard_map/all_gather | solution.py:145
  608.4 15.6 fusion.247
  645.5 15.8 fusion.250
  683.8 28.9 %all-gather.71.cloned.1.call-done = bf16[1024,1088]{0,1:T(8,128)(2,1)} async-done(((bf16[256,1088]{0,1:T(8,128)(2,1)}), bf16[1024,1088]{0,1:T(8,128)(2,1)}) %all-gather.71.cloned.1.call-update) | async-done | bytes 2228240 | tf_op jit(solution)/shard_map/all_gather | solution.py:144
  728.9 21.8 %all-gather.69.cloned.1.call-done = bf16[1024,1088]{0,1:T(8,128)(2,1)} async-done(((bf16[256,1088]{0,1:T(8,128)(2,1)}), bf16[1024,1088]{0,1:T(8,128)(2,1)}) %all-gather.69.cloned.1.call-update) | async-done | bytes 2228240 | tf_op jit(solution)/shard_map/all_gather | solution.py:145
  875.3 15.6 fusion.255
  1009.0 15.8 fusion.260
  1024.8 17.2 maximum_maximum_fusion
  1058.5 28.1 %all-to-all-done = bf16[768,4,272]{0,2,1:T(8,128)(2,1)S(1)} async-done(((bf16[768,4,272]{0,2,1:T(8,128)(2,1)}), bf16[768,4,272]{0,2,1:T(8,128)(2,1)S(1)}, u32[]{:S(2)}, u32[]{:S(2)}) %all-to-all-start) | async-done | bytes 1671200 | tf_op jit(solution)/shard_map/all_to_all | solution.py:352
  1093.5 35.2 %all-to-all-done.2 = bf16[768,4,272]{0,2,1:T(8,128)(2,1)} async-done(((bf16[768,4,272]{0,2,1:T(8,128)(2,1)}), bf16[768,4,272]{0,2,1:T(8,128)(2,1)}, u32[]{:S(2)}, u32[]{:S(2)}) %all-to-all-start.2) | async-done | bytes 1671200 | tf_op jit(solution)/shard_map/all_to_all | solution.py:354
  1176.2 119.7 %all-to-all-done.3 = bf16[768,4,1088]{0,2,1:T(8,128)(2,1)} async-done(((bf16[768,4,1088]{0,2,1:T(8,128)(2,1)}), bf16[768,4,1088]{0,2,1:T(8,128)(2,1)}, u32[]{:S(2)}, u32[]{:S(2)}) %all-to-all-start.3) | async-done | bytes 6684704 | tf_op jit(solution)/shard_map/all_to_all | solution.py:355
  1328.0 83.2 %all-gather.53.cloned.1.call-done = bf16[3072,3264]{0,1:T(8,128)(2,1)} async-done(((bf16[768,3264]{0,1:T(8,128)(2,1)}), bf16[3072,3264]{0,1:T(8,128)(2,1)}) %all-gather.53.cloned.1.call-update) | async-done | bytes 20054032 | tf_op jit(solution)/shard_map/all_gather | solution.py:360
  1422.9 230.7 %all-gather.57.cloned.1.call-done = bf16[3072,4352]{1,0:T(8,128)(2,1)} async-done(((bf16[768,4352]{1,0:T(8,128)(2,1)}), bf16[3072,4352]{1,0:T(8,128)(2,1)}) %all-gather.57.cloned.1.call-update) | async-done | bytes 26738704 | tf_op jit(solution)/shard_map/all_gather | solution.py:358
  1688.8 17.7 all-reduce.11
  1721.5 20.1 %all-reduce.13 = (bf16[1,272]{1,0:T(2,128)(2,1)S(1)}, bf16[1,272]{1,0:T(2,128)(2,1)S(1)}, bf16[1,272]{1,0:T(2,128)(2,1)S(1)}, bf16[1,272]{1,0:T(2,128)(2,1)S(1)}...) all-reduce(bf16[1,272]{1,0:T(2,128)(2,1)S(1)} %dynamic-slice_conver, ...), channel_id=1, replica_groups=mesh['section'=2,'replica'=4,'shard'=4] {'replica'}, use_global_device_ids=true, to_apply=%region_49.50 | all-reduce | flops 2720 | bytes 10880 | tf_op jit(solution)/shard_map/psum | solution.py:403
  1745.6 180.0 %all-reduce.17.cloned.1.call-done = (bf16[1,272,3264]{2,1,0:T(8,128)(2,1)}, bf16[1,272,1088]{2,1,0:T(8,128)(2,1)}, bf16[1,272,4352]{2,1,0:T(8,128)(2,1)}, bf16[1,1088,1088]{2,1,0:T(8,128)(2,1)}) async-done(((bf16[1,272,3264]{2,1,0:T(8,128)(2,1)}, bf16[1,272,1088]{2,1,0:T(8,128)(2,1)}, bf16[1,272,4352]{2,1,0:T(8,128)(2,1)}, bf16[1,1088,1088]{2,1,0:T(8,128)(2,1)}), (bf16[1,272,3264]{2,1,0:T(8,128)(2,1)}, ...) | async-done | bytes 7102480 | tf_op jit(solution)/shard_map/psum | solution.py:405
  (607 shorter events, 678.7 us)
Async XLA Ops:
  7.2 84.3 %all-gather.33.cloned.1.call-start = ((), (), s32[]{:S(2)}) async-start(), calls=%async_computation.4 | async-start | bytes 9052160 | tf_op jit(solution)/shard_map/all_gather | solution.py:82
  7.9 128.9 %all-gather.63.cloned.1.call-start = ((), (), s32[]{:S(2)}) async-start(), calls=%async_computation.19 | async-start | bytes 2785280 | tf_op jit(solution)/shard_map/all_gather | solution.py:144
  100.4 75.1 %all-gather.61.cloned.1.call-start = ((), (), s32[]{:S(2)}) async-start(), calls=%async_computation.18 | async-start | bytes 2785280 | tf_op jit(solution)/shard_map/all_gather | solution.py:145
  101.1 114.8 %all-gather.35.cloned.1.call-start = ((), (), s32[]{:S(2)}) async-start(), calls=%async_computation.5 | async-start | bytes 3133440 | tf_op jit(solution)/shard_map/all_gather | solution.py:83
  101.7 212.5 %all-gather.37.cloned.1.call-start = ((), (), s32[]{:S(2)}) async-start(), calls=%async_computation.6 | async-start | bytes 11837440 | tf_op jit(solution)/shard_map/all_gather | solution.py:87
  102.3 314.9 %all-gather.39.cloned.1.call-start = ((), (), s32[]{:S(2)}) async-start(), calls=%async_computation.7 | async-start | bytes 12533760 | tf_op jit(solution)/shard_map/all_gather | solution.py:89
  102.9 374.5 %all-gather.67.cloned.1.call-start = ((), (), s32[]{:S(2)}) async-start(), calls=%async_computation.21 | async-start | bytes 2785280 | tf_op jit(solution)/shard_map/all_gather | solution.py:144
  440.9 75.1 %all-gather.65.cloned.1.call-start = ((), (), s32[]{:S(2)}) async-start(), calls=%async_computation.20 | async-start | bytes 2785280 | tf_op jit(solution)/shard_map/all_gather | solution.py:145
  441.7 182.3 %all-gather.41.cloned.1.call-start = ((), (), s32[]{:S(2)}) async-start(), calls=%async_computation.8 | async-start | bytes 2785280 | tf_op jit(solution)/shard_map/all_gather | solution.py:273
  445.9 189.4 %all-gather.43.cloned.1.call-start = ((), (), s32[]{:S(2)}) async-start(), calls=%async_computation.9 | async-start | bytes 2785280 | tf_op jit(solution)/shard_map/all_gather | solution.py:274
  544.6 89.7 %collective-permute-start.1 = (bf16[1,256,1088]{1,2,0:T(8,128)(2,1)}, bf16[1,256,1088]{1,2,0:T(8,128)(2,1)}, u32[]{:S(2)}, u32[]{:S(2)}) collective-permute-start(bf16[1,256,1088]{1,2,0:T(8,128)(2,1)} %bitcast.684), channel_id=1, source_target_pairs={{0,16},{1,17},{2,18},{3,19},{4,20},{5,21},{6,22},{7,23},{8,24},{9,... | collective-permute-start | bytes 1671176 | tf_op jit(solution)/shard_map/ppermute | solution.py:17
  575.9 136.8 %all-gather.71.cloned.1.call-start = ((), (), s32[]{:S(2)}) async-start(), calls=%async_computation.23 | async-start | bytes 2785280 | tf_op jit(solution)/shard_map/all_gather | solution.py:144
  676.6 74.1 %all-gather.69.cloned.1.call-start = ((), (), s32[]{:S(2)}) async-start(), calls=%async_computation.22 | async-start | bytes 2785280 | tf_op jit(solution)/shard_map/all_gather | solution.py:145
  677.2 177.7 %all-gather.45.cloned.1.call-start = ((), (), s32[]{:S(2)}) async-start(), calls=%async_computation.10 | async-start | bytes 2785280 | tf_op jit(solution)/shard_map/all_gather | solution.py:273
  680.7 97.2 %collective-permute-start.2 = (bf16[1,256,1088]{1,2,0:T(8,128)(2,1)}, bf16[1,256,1088]{1,2,0:T(8,128)(2,1)}, u32[]{:S(2)}, u32[]{:S(2)}) collective-permute-start(bf16[1,256,1088]{1,2,0:T(8,128)(2,1)} %bitcast.67), channel_id=1, source_target_pairs={{16,0},{17,1},{18,2},{19,3},{20,4},{21,5},{22,6},{23,7},{24,8},{25... | collective-permute-start | bytes 1671176 | tf_op jit(solution)/shard_map/ppermute | solution.py:17
  683.8 181.7 %all-gather.47.cloned.1.call-start = ((), (), s32[]{:S(2)}) async-start(), calls=%async_computation.11 | async-start | bytes 2785280 | tf_op jit(solution)/shard_map/all_gather | solution.py:274
  793.5 156.9 %all-gather.49.cloned.1.call-start = ((), (), s32[]{:S(2)}) async-start(), calls=%async_computation.12 | async-start | bytes 2785280 | tf_op jit(solution)/shard_map/all_gather | solution.py:273
  794.1 203.9 %all-gather.51.cloned.1.call-start = ((), (), s32[]{:S(2)}) async-start(), calls=%async_computation.13 | async-start | bytes 2785280 | tf_op jit(solution)/shard_map/all_gather | solution.py:274
  924.2 382.1 %all-gather.55.cloned.1.call-start = ((), (), s32[]{:S(2)}) async-start(), calls=%async_computation.15 | async-start | bytes 8355840 | tf_op jit(solution)/shard_map/all_gather | solution.py:359
  926.8 386.9 %all-gather.59.cloned.1.call-start = ((), (), s32[]{:S(2)}) async-start(), calls=%async_computation.17 | async-start | bytes 8355840 | tf_op jit(solution)/shard_map/all_gather | solution.py:357
  930.8 480.3 %all-gather.53.cloned.1.call-start = ((), (), s32[]{:S(2)}) async-start(), calls=%async_computation.14 | async-start | bytes 25067520 | tf_op jit(solution)/shard_map/all_gather | solution.py:360
  1042.0 611.5 %all-gather.57.cloned.1.call-start = ((), (), s32[]{:S(2)}) async-start(), calls=%async_computation.16 | async-start | bytes 33423360 | tf_op jit(solution)/shard_map/all_gather | solution.py:358
  1164.5 131.4 %all-to-all-start.3 = ((bf16[768,4,1088]{0,2,1:T(8,128)(2,1)}), bf16[768,4,1088]{0,2,1:T(8,128)(2,1)}, u32[]{:S(2)}, u32[]{:S(2)}) async-start(bf16[768,4,1088]{0,2,1:T(8,128)(2,1)} %bitcast.613), calls=%async_computation.3 | async-start | bytes 13369344 | tf_op jit(solution)/shard_map/all_to_all | solution.py:355
  1169.8 755.8 %all-reduce.17.cloned.1.call-start = ((), (), s32[]{:S(2)}) async-start(), calls=%async_computation.24 | async-start | bytes 14622720 | tf_op jit(solution)/shard_map/psum | solution.py:405
  (166 other events, 6020.0 us)
Sparse Core Ops, SparseCore 0:
  9.9 81.5 all-gather.32
  100.5 36.2 all-gather.62
  139.2 36.2 all-gather.60
  177.2 38.6 all-gather.34
  217.6 96.5 all-gather.36
  316.0 101.2 all-gather.38
  441.1 36.2 all-gather.66
  479.8 36.2 all-gather.64
  517.9 36.2 all-gather.40
  576.0 37.0 all-gather.42
  676.8 35.9 all-gather.70
  714.4 36.2 all-gather.68
  752.5 36.2 all-gather.44
  793.6 36.3 all-gather.46
  831.7 36.2 all-gather.48
  924.3 37.5 all-gather.50
  963.5 74.2 all-gather.54
  1039.5 125.0 all-gather.58
  1167.1 243.9 all-gather.52
  1412.8 240.6 all-gather.56
  1667.9 257.6 all-reduce.16
where the time goes:
time: 1950 us; the launch traced here: 1940 us
  waiting for transfers between devices  1130 us (58%)
  matrix products  461 us (24%)
  other arithmetic  127 us (7%)
  blocking collectives  107 us (5%)
  local copies, waits for them, and re-layouts  70.3 us (4%)
  starting transfers between devices  26.7 us (1%)
    all_gather x1, waiting for transfers between devices, local(): piece_gate = lax.all_gather(grads_of(1), 'shard', axis=0, tiled=True)  231 us
    psum x1, waiting for transfers between devices, local(): lax.psum(shares[2].astype(jnp.bfloat16), 'replica').astype(jnp.float32)  180 us
    all_to_all x1, waiting for transfers between devices, local(): lax.all_to_all(stacked('activated'), 'shard', split_axis=1, concat_axis=0...  120 us
    all_gather x1, waiting for transfers between devices, local(): lax.all_gather(params[7], 'shard', axis=1, tiled=True)  95.2 us
    all_gather x1, waiting for transfers between devices, local(): lax.all_gather(params[9], 'shard', axis=1, tiled=True)  93.8 us
    all_gather x3, waiting for transfers between devices, local(): lax.all_gather(forward_keys_local, 'shard', axis=1, tiled=True)  91.4 us
    all_gather x1, waiting for transfers between devices, local(): piece_project = lax.all_gather(grads_of(3), 'shard', axis=0, tiled=True)  83.2 us
    dot_general x9, matrix products, attend_scores(): jnp.einsum('sqhd,skhd->shqk', query_heads, key_heads, preferred_element_t...  74 us
  transfers between devices with their start and end apart: 29, of which 19 were waited for; matrix products, arithmetic and copies ran while one was open for 27% of the time, Pallas kernels for 0%

commit v1 on v0

v1 whole, which is shorter than its diff:
```python
import functools
import math

import jax
import jax.numpy as jnp
from jax import lax
from jax.experimental import pallas as pl
from jax.experimental.pallas import tpu as pltpu
from jax.sharding import PartitionSpec as P

HD = 64
QUERY_BLOCK = 128

norm_eps = 1e-05
LOW = jnp.bfloat16
WIDE = jnp.float32


def layer_norm(values, gain, bias):
    centre = jnp.mean(values, -1, keepdims=True)
    centered = values - centre
    spread = jnp.mean(centered * centered, -1, keepdims=True)
    return centered * lax.rsqrt(spread + norm_eps) * gain + bias


def smooth_gate(values):
    return jax.nn.gelu(values, approximate=True)


def times(left, right):
    return jnp.dot(left, right, preferred_element_type=WIDE)


def contract_rows(left, right):
    return lax.dot_general(
        left, right, (((0,), (0,)), ((), ())), preferred_element_type=WIDE
    )


def times_transpose(left, right):
    return lax.dot_general(
        left, right, (((1,), (1,)), ((), ())), preferred_element_type=WIDE
    )


def fill_order(place, span, pieces, scratch, offset, count, factor=None):
    for k, piece in enumerate(pieces):
        rows = pl.ds(pl.multiple_of((place ^ k) * span, span), span)
        for h in range(count):
            part = piece[:, offset + h * HD : offset + (h + 1) * HD]
            if factor is not None:
                part = part * jnp.asarray(factor, part.dtype)
            scratch[h, rows, :] = part


def write_mask(mask_ref, seg_row_ref, seg_col_ref, start, block, reach):
    same = seg_col_ref[start : start + block, :] == seg_row_ref[:, :reach]
    row = lax.broadcasted_iota(jnp.int32, (block, reach), 0) + start
    col = lax.broadcasted_iota(jnp.int32, (block, reach), 1)
    mask_ref[:, :reach] = jnp.where(same & (col <= row), 0.0, -1e30)


def mix_forward_kernel(count, span, scale, place_ref, seg_row_ref, seg_col_ref, *refs):
    shards = len(refs) // 2 - 3
    pieces = refs[:shards]
    outs = refs[shards : 2 * shards]
    lse_ref, q_s, k_s, v_s, o_s, mask_ref = refs[2 * shards :]
    place = place_ref[0]
    wide = count * HD
    fill_order(place, span, pieces, q_s, 0, count, scale)
    fill_order(place, span, pieces, k_s, wide, count)
    fill_order(place, span, pieces, v_s, 2 * wide, count)
    length = q_s.shape[1]
    block = min(QUERY_BLOCK, length)
    lane = lax.broadcasted_iota(jnp.int32, (block, 128), 1)
    for start in range(0, length, block):
        reach = start + block
        write_mask(mask_ref, seg_row_ref, seg_col_ref, start, block, reach)
        lse_ref[start:reach, :] = jnp.zeros((block, 128), WIDE)

        @pl.loop(0, count)
        def _(h):
            q = q_s[h, start:reach, :]
            scores = times_transpose(q, k_s[h, :reach, :]) + mask_ref[:, :reach]
            peak = jnp.max(scores, -1, keepdims=True)
            raised = jnp.exp(scores - peak)
            total = jnp.sum(raised, -1, keepdims=True)
            mixed = times(raised.astype(LOW), v_s[h, :reach, :])
            o_s[h, start:reach, :] = (mixed * (1.0 / total)).astype(LOW)
            lse_ref[start:reach, :] = jnp.where(
                lane == h, peak + jnp.log(total), lse_ref[start:reach, :]
            )

    for k, out in enumerate(outs):
        rows = pl.ds(pl.multiple_of((place ^ k) * span, span), span)
        for h in range(count):
            out[:, h * HD : (h + 1) * HD] = o_s[h, rows, :]


def mix_backward_kernel(count, span, scale, place_ref, seg_row_ref, seg_col_ref, lse_ref, *refs):
    shards = (len(refs) - 8) // 3
    pieces = refs[:shards]
    grads = refs[shards : 2 * shards]
    outs = refs[2 * shards : 3 * shards]
    q_s, k_s, v_s, g_s, dq_s, dk_s, dv_s, mask_ref = refs[3 * shards :]
    place = place_ref[0]
    wide = count * HD
    fill_order(place, span, pieces, q_s, 0, count, scale)
    fill_order(place, span, pieces, k_s, wide, count)
    fill_order(place, span, pieces, v_s, 2 * wide, count)
    fill_order(place, span, grads, g_s, 0, count)
    dk_s[...] = jnp.zeros_like(dk_s)
    dv_s[...] = jnp.zeros_like(dv_s)
    length = q_s.shape[1]
    block = min(QUERY_BLOCK, length)
    lane = lax.broadcasted_iota(jnp.int32, (block, 128), 1)
    for start in range(0, length, block):
        reach = start + block
        write_mask(mask_ref, seg_row_ref, seg_col_ref, start, block, reach)

        @pl.loop(0, count)
        def _(h):
            q = q_s[h, start:reach, :]
            g = g_s[h, start:reach, :]
            keys = k_s[h, :reach, :]
            lse = jnp.sum(
                jnp.where(lane == h, lse_ref[start:reach, :], 0.0), -1, keepdims=True
            )
            scores = times_transpose(q, keys) + mask_ref[:, :reach]
            probs = jnp.exp(scores - lse)
            grad_probs = times_transpose(g, v_s[h, :reach, :])
            inner = jnp.sum(probs * grad_probs, -1, keepdims=True)
            grad_scores = (probs * (grad_probs - inner)).astype(LOW)
            dq_s[h, start:reach, :] = (times(grad_scores, keys) * scale).astype(LOW)
            dk_s[h, :reach, :] += contract_rows(grad_scores, q)
            dv_s[h, :reach, :] += contract_rows(probs.astype(LOW), g)

    for k, out in enumerate(outs):
        rows = pl.ds(pl.multiple_of((place ^ k) * span, span), span)
        for h in range(count):
            out[:, h * HD : (h + 1) * HD] = dq_s[h, rows, :]
            out[:, wide + h * HD : wide + (h + 1) * HD] = dk_s[h, rows, :].astype(LOW)
            out[:, 2 * wide + h * HD : 2 * wide + (h + 1) * HD] = dv_s[h, rows, :].astype(LOW)


def in_vmem(amount):
    return [pl.BlockSpec(memory_space=pltpu.VMEM)] * amount


def mix_forward(place, segment, pieces, count):
    shards = len(pieces)
    span = pieces[0].shape[0]
    length = segment.shape[0]
    scale = 1.0 / math.sqrt(HD)
    block = min(QUERY_BLOCK, length)
    outs = pl.pallas_call(
        functools.partial(mix_forward_kernel, count, span, scale),
        out_shape=[jax.ShapeDtypeStruct((span, count * HD), LOW)] * shards
        + [jax.ShapeDtypeStruct((length, 128), WIDE)],
        in_specs=[pl.BlockSpec(memory_space=pltpu.SMEM)] + in_vmem(2 + shards),
        out_specs=in_vmem(shards + 1),
        scratch_shapes=[pltpu.VMEM((count, length, HD), LOW)] * 4
        + [pltpu.VMEM((block, length), WIDE)],
        compiler_params=pltpu.CompilerParams(vmem_limit_bytes=40 << 20),
        cost_estimate=pl.CostEstimate(
            flops=count * length * length * HD * 8,
            bytes_accessed=8 * length * count * HD,
            transcendentals=count * length * length,
        ),
        name="mix_forward",
    )(place.reshape(1), segment.reshape(1, length), segment.reshape(length, 1), *pieces)
    return outs[:shards], outs[shards]


def mix_backward(place, segment, lse, pieces, grads, count):
    shards = len(pieces)
    span = pieces[0].shape[0]
    length = segment.shape[0]
    scale = 1.0 / math.sqrt(HD)
    block = min(QUERY_BLOCK, length)
    return pl.pallas_call(
        functools.partial(mix_backward_kernel, count, span, scale),
        out_shape=[jax.ShapeDtypeStruct((span, 3 * count * HD), LOW)] * shards,
        in_specs=[pl.BlockSpec(memory_space=pltpu.SMEM)] + in_vmem(3 + 2 * shards),
        out_specs=in_vmem(shards),
        scratch_shapes=[pltpu.VMEM((count, length, HD), LOW)] * 5
        + [pltpu.VMEM((count, length, HD), WIDE)] * 2
        + [pltpu.VMEM((block, length), WIDE)],
        compiler_params=pltpu.CompilerParams(vmem_limit_bytes=40 << 20),
        cost_estimate=pl.CostEstimate(
            flops=count * length * length * HD * 20,
            bytes_accessed=16 * length * count * HD,
            transcendentals=count * length * length,
        ),
        name="mix_backward",
    )(
        place.reshape(1),
        segment.reshape(1, length),
        segment.reshape(length, 1),
        lse,
        *pieces,
        *grads,
    )


def exchange(pieces):
    shards = len(pieces)
    return [pieces[0]] + [
        lax.ppermute(pieces[k], "shard", [(i, i ^ k) for i in range(shards)])
        for k in range(1, shards)
    ]


def swap(block):
    return lax.ppermute(block, "section", [(0, 1), (1, 0)])


def in_order(blocks, place, axis):
    size = blocks[0].shape[axis]
    shape = list(blocks[0].shape)
    shape[axis] = size * len(blocks)
    whole = jnp.zeros(shape, blocks[0].dtype)
    for k, block in enumerate(blocks):
        whole = lax.dynamic_update_slice_in_dim(whole, block, (place ^ k) * size, axis)
    return whole


def to_layer_owner(block, layer):
    moved = lax.ppermute(block, "section", [(1 - layer, layer)])
    return block.astype(WIDE) + moved.astype(WIDE)


def sum_replicas(block, layer):
    dtype = block.dtype
    replicas = lax.axis_size("replica")
    if replicas != 4:
        return lax.psum(block, "replica").astype(WIDE)
    base = layer * replicas
    axes = ("section", "replica")

    def move(value, route):
        return lax.ppermute(value, axes, [(base + a, base + b) for a, b in route])

    inward = move(block, [(0, 1), (3, 2)])
    half = (block.astype(WIDE) + inward.astype(WIDE)).astype(dtype)
    across = move(half, [(1, 2), (2, 1)])
    total = (half.astype(WIDE) + across.astype(WIDE)).astype(dtype)
    outward = move(total, [(1, 0), (2, 3)])
    place = lax.axis_index("replica")
    return jnp.where((place == 0) | (place == 3), outward, total).astype(WIDE)


def local(
    inputs,
    cotangent,
    segments,
    ln1_gain,
    ln1_bias,
    w_qkv,
    w_out,
    out_bias,
    ln2_gain,
    ln2_bias,
    w_up,
    up_bias,
    w_down,
    down_bias,
):
    first = lax.axis_index("section") == 0
    place = lax.axis_index("shard")
    shards = lax.axis_size("shard")
    span, width = inputs.shape[2:]
    length = segments.shape[2]
    heads = width // HD
    count = -(-heads // shards)
    mine_wide = count * HD
    own_rows = ln1_gain.shape[1]
    own_hidden = up_bias.shape[1]
    hidden_rows = own_hidden // own_rows
    partners = range(shards)

    def pick(pair):
        return jnp.where(first, pair[0], pair[1])

    def by_layer(mine):
        other = swap(mine)
        return (jnp.where(first, mine, other), jnp.where(first, other, mine))

    fresh = pick((inputs[0, 0], inputs[1, 0]))
    segment = pick((segments[0, 0], segments[1, 0]))
    grad_last = pick((cotangent[0, 0], cotangent[1, 0]))

    vectors = jnp.concatenate(
        [ln1_gain, ln1_bias, out_bias, ln2_gain, ln2_bias, down_bias]
        + [up_bias.reshape(hidden_rows, own_rows)],
        0,
    )
    vectors = lax.all_gather(vectors, ("section", "shard"))
    vectors = vectors.reshape(2, shards, 6 + hidden_rows, own_rows)
    small = vectors[:, :, :6].transpose(0, 2, 1, 3).reshape(2, 6, width).astype(WIDE)
    hidden_bias = (
        lax.dynamic_index_in_dim(vectors, place, 1, False)[:, 6:]
        .reshape(2, own_hidden)
        .astype(WIDE)
    )

    qkv_columns = jnp.pad(
        w_qkv[0].reshape(own_rows, 3, width), ((0, 0), (0, 0), (0, shards * mine_wide - width))
    )
    qkv_pieces = [
        lax.dynamic_slice_in_dim(qkv_columns, (place ^ k) * mine_wide, mine_wide, 2).reshape(
            own_rows, 3 * mine_wide
        )
        for k in partners
    ]
    proj_qkv = by_layer(in_order(exchange(qkv_pieces), place, 0))
    chunks_first = exchange([fresh] * shards)
    proj_out = by_layer(in_order(exchange([w_out[0]] * shards), place, 0))
    up_pieces = [
        lax.dynamic_slice_in_dim(w_up[0], (place ^ k) * own_hidden, own_hidden, 1)
        for k in partners
    ]
    proj_up = by_layer(in_order(exchange(up_pieces), place, 0))
    proj_down = by_layer(w_down[0])

    def forward(layer, low_hidden, chunks):
        gain_one, bias_one, bias_out, gain_two, bias_two, bias_down = small[layer]
        normed = [
            layer_norm(chunk.astype(WIDE), gain_one, bias_one).astype(LOW) for chunk in chunks
        ]
        project = [times(chunk, proj_qkv[layer]).astype(LOW) for chunk in normed]
        mixed_parts, lse = mix_forward(place, segment, project, count)
        mixed = in_order(exchange(mixed_parts), place, 1)[:, :width]
        hidden = low_hidden.astype(WIDE)
        middle = hidden + times(mixed, proj_out[layer]) + bias_out
        normed_two = exchange(
            [layer_norm(middle, gain_two, bias_two).astype(LOW)] * shards
        )
        gate_in = [times(chunk, proj_up[layer]) + hidden_bias[layer] for chunk in normed_two]
        activated = [smooth_gate(chunk).astype(LOW) for chunk in gate_in]
        terms = [times(chunk, proj_down[layer]) for chunk in activated]
        terms = exchange([terms[0]] + [term.astype(LOW) for term in terms[1:]])
        result = middle + bias_down + sum(term.astype(WIDE) for term in terms)
        saved = (hidden, normed, project, lse, mixed, middle, normed_two, gate_in, activated)
        return result.astype(LOW), saved

    def backward(layer, grad_low, branch, saved):
        hidden, normed, project, lse, mixed, middle, normed_two, gate_in, activated = saved
        gain_one, bias_one, bias_out, gain_two, bias_two, bias_down = small[layer]
        grad_out = grad_low.astype(WIDE)
        grad_gate = [
            jax.vjp(smooth_gate, gate)[1](times_transpose(chunk, proj_down[layer]))[0].astype(LOW)
            for chunk, gate in zip(branch, gate_in)
        ]
        terms = [times_transpose(chunk, proj_up[layer]) for chunk in grad_gate]
        terms = exchange([terms[0]] + [term.astype(LOW) for term in terms[1:]])
        grad_normed_two = sum(term.astype(WIDE) for term in terms)
        norm_pull_two = jax.vjp(layer_norm, middle, gain_two, bias_two)[1]
        grad_mid, grad_gain_two, grad_bias_two = norm_pull_two(grad_normed_two)
        grad_middle = grad_out + grad_mid
        grad_attn = grad_middle.astype(LOW)
        grad_mixed = jnp.pad(
            times_transpose(grad_attn, proj_out[layer]).astype(LOW),
            ((0, 0), (0, shards * mine_wide - width)),
        )
        grad_mixed = exchange(
            [
                lax.dynamic_slice_in_dim(grad_mixed, (place ^ k) * mine_wide, mine_wide, 1)
                for k in partners
            ]
        )
        grad_project = mix_backward(place, segment, lse, project, grad_mixed, count)
        terms = [times_transpose(chunk, proj_qkv[layer]) for chunk in grad_project]
        terms = exchange([terms[0]] + [term.astype(LOW) for term in terms[1:]])
        grad_normed = sum(term.astype(WIDE) for term in terms)
        norm_pull_one = jax.vjp(layer_norm, hidden, gain_one, bias_one)[1]
        grad_hidden, grad_gain_one, grad_bias_one = norm_pull_one(grad_normed)
        grad_input = (grad_middle + grad_hidden).astype(LOW)

        def rows_product(left, right):
            return contract_rows(jnp.concatenate(left, 0), jnp.concatenate(right, 0)).astype(LOW)

        down_sum = to_layer_owner(rows_product(activated, branch), layer).astype(LOW)
        down_sum = sum_replicas(down_sum, layer)

        def rows_to_owner(value):
            value = to_layer_owner(value, layer).astype(LOW)
            return exchange(
                [
                    lax.dynamic_slice_in_dim(value, (place ^ k) * own_rows, own_rows, 0)
                    for k in partners
                ]
            )

        up_sum = [
            sum_replicas(piece, layer)
            for piece in rows_to_owner(rows_product(normed_two, grad_gate))
        ]
        out_terms = rows_to_owner(contract_rows(mixed, grad_attn).astype(LOW))
        out_sum = sum_replicas(sum(term.astype(WIDE) for term in out_terms).astype(LOW), layer)
        qkv_sum = [
            sum_replicas(piece, layer)
            for piece in rows_to_owner(rows_product(normed, grad_project))
        ]
        vector_terms = jnp.stack(
            [
                grad_gain_one,
                grad_bias_one,
                jnp.sum(grad_attn.astype(WIDE), 0),
                grad_gain_two,
                grad_bias_two,
                jnp.sum(grad_low.astype(WIDE), 0),
            ]
        )
        vector_terms = sum(
            exchange(
                [
                    lax.dynamic_slice_in_dim(vector_terms, (place ^ k) * own_rows, own_rows, 1)
                    for k in partners
                ]
            )
        )
        up_terms = sum(jnp.sum(chunk.astype(WIDE), 0) for chunk in grad_gate)
        vector_terms = jnp.concatenate(
            [vector_terms, up_terms.reshape(hidden_rows, own_rows)], 0
        )
        vector_sum = sum_replicas(to_layer_owner(vector_terms, layer), layer)
        return grad_input, (down_sum, up_sum, out_sum, qkv_sum, vector_sum)

    branch_last = exchange([grad_last] * shards)
    sent, saved_first = forward(0, fresh, chunks_first)
    chunks_second = exchange([sent] * shards)
    final, saved_second = forward(1, sent, chunks_second)
    grad_sent, sums_second = backward(1, grad_last, branch_last, saved_second)
    branch_first = exchange([grad_sent] * shards)
    grad_first, sums_first = backward(0, grad_sent, branch_first, saved_first)

    def both_micro(of_first, of_second):
        own = jnp.where(first, of_first, of_second)
        moved = swap(jnp.where(first, of_second, of_first))
        return jnp.where(first, jnp.stack([own, moved]), jnp.stack([moved, own]))[None, :, None]

    section_outputs = both_micro(sent, final)
    input_grads = both_micro(grad_first, grad_sent)

    down_sum, up_sum, out_sum, qkv_sum, vector_sum = jax.tree.map(
        lambda a, b: jnp.where(first, a, b), sums_first, sums_second
    )
    up_sum = in_order(up_sum, place, 1)
    qkv_sum = in_order(
        [piece.reshape(own_rows, 3, mine_wide) for piece in qkv_sum], place, 2
    )[:, :, :width].reshape(own_rows, 3 * width)
    return (
        section_outputs,
        input_grads,
        vector_sum[0:1],
        vector_sum[1:2],
        qkv_sum[None],
        out_sum[None],
        vector_sum[2:3],
        vector_sum[3:4],
        vector_sum[4:5],
        up_sum[None],
        vector_sum[6:].reshape(1, own_hidden),
        down_sum[None],
        vector_sum[5:6],
    )


def solution(mesh):
    return jax.shard_map(
        local,
        mesh=mesh,
        in_specs=(
            P(None, "replica", "shard", None),
            P(None, "replica", "shard", None),
            P(None, "replica", None),
            P("section", "shard"),
            P("section", "shard"),
            P("section", "shard", None),
            P("section", "shard", None),
            P("section", "shard"),
            P("section", "shard"),
            P("section", "shard"),
            P("section", "shard", None),
            P("section", "shard"),
            P("section", "shard", None),
            P("section", "shard"),
        ),
        out_specs=(
            P("section", None, "replica", "shard", None),
            P("section", None, "replica", "shard", None),
            P("section", "shard"),
            P("section", "shard"),
            P("section", "shard", None),
            P("section", "shard", None),
            P("section", "shard"),
            P("section", "shard"),
            P("section", "shard"),
            P("section", "shard", None),
            P("section", "shard"),
            P("section", "shard", None),
            P("section", "shard"),
        ),
        check_vma=False,
    )
```

time: 1950 us -> 1400 us (0.72)
  waiting for transfers between devices: 1130 us -> 369 us
  matrix products: 461 us -> 143 us
  local copies, waits for them, and re-layouts: 70.3 us -> 369 us
  starting transfers between devices: 26.7 us -> 245 us
  Pallas kernels: 0 us -> 93.6 us
  blocking collectives: 107 us -> 40.5 us
    all_gather x20 -> x0, waiting for transfers between devices: 745 us -> none  [the longest x1 231 us: local(): piece_gate = lax.all_gather(grads_of(1), 'shard', axis=0, tiled=True)]
    ppermute x4 -> x163, waiting for transfers between devices: 3.44 us -> 369 us  [the longest x81 247 us: exchange(): lax.ppermute(pieces[k], 'shard', [(i, i ^ k) for i in range(shards)])]
    dot_general x36 -> x26, matrix products: 350 us -> 47.8 us  [times(): return jnp.dot(left, right, preferred_element_type=WIDE)]
    dynamic_update_slice x0 -> x28, local copies, waits for them, and re-layouts: none -> 244 us  [in_order(): lax.dynamic_update_slice_in_dim(whole, block, (place ^ k) * size, axis)]
    ppermute x4 -> x163, starting transfers between devices: 7.55 us -> 245 us  [the longest x81 106 us: exchange(): lax.ppermute(pieces[k], 'shard', [(i, i ^ k) for i in range(shards)])]
    all_to_all x4 -> x0, waiting for transfers between devices: 198 us -> none  [the longest x1 120 us: local(): lax.all_to_all(stacked('activated'), 'shard', split_axis=1, concat_axis=0...]
    psum x1 -> x0, waiting for transfers between devices: 180 us -> none  [local(): lax.psum(shares[2].astype(jnp.bfloat16), 'replica').astype(jnp.float32)]
    pallas_call x0 -> x4, Pallas kernels: none -> 93.6 us  [the longest x2 53.4 us: mix_backward(): pl.pallas_call(functools.partial(mix_backward_kernel, count, span, scale)...]
  transfers between devices with their start and end apart: 29 -> 163, of which waited for: 19 -> 52; matrix products, arithmetic and copies ran while one was open for 27% -> 45% of each run, Pallas kernels for 0% -> 7%
where the time goes in v1:
time: 1400 us; the launch traced here: 1390 us
  local copies, waits for them, and re-layouts  369 us (26%)
  waiting for transfers between devices  369 us (26%)
  starting transfers between devices  245 us (18%)
  matrix products  143 us (10%)
  other arithmetic  124 us (9%)
  Pallas kernels  93.6 us (7%)
  blocking collectives  40.5 us (3%)
    ppermute x81, waiting for transfers between devices, exchange(): lax.ppermute(pieces[k], 'shard', [(i, i ^ k) for i in range(shards)])  247 us
    dynamic_update_slice x28, local copies, waits for them, and re-layouts, in_order(): lax.dynamic_update_slice_in_dim(whole, block, (place ^ k) * size, axis)  244 us
    ppermute x66, waiting for transfers between devices, move(): return lax.ppermute(value, axes, [(base + a, base + b) for a, b in route])  118 us
    ppermute x81, starting transfers between devices, exchange(): lax.ppermute(pieces[k], 'shard', [(i, i ^ k) for i in range(shards)])  106 us
    ppermute x66, starting transfers between devices, move(): return lax.ppermute(value, axes, [(base + a, base + b) for a, b in route])  103 us
    dot_general x26, matrix products, times_transpose(): lax.dot_general(left, right, (((1,), (1,)), ((), ())), preferred_element_...  60.6 us
    pallas_call x2, Pallas kernels, mix_backward(): pl.pallas_call(functools.partial(mix_backward_kernel, count, span, scale)...  53.4 us
    dot_general x26, matrix products, times(): return jnp.dot(left, right, preferred_element_type=WIDE)  47.8 us
  transfers between devices with their start and end apart: 163, of which 52 were waited for; matrix products, arithmetic and copies ran while one was open for 45% of the time, Pallas kernels for 7%

profile of v1, /device:TPU:0, one launch (start us, length us, event | category | flops | bytes accessed | tf_op | source)
XLA Modules:
  0.0 1389.2 jit_solution(9401236913715618155)
XLA Ops:
  32.7 40.5 %all-gather.1 = bf16[8,10,272]{2,1,0:T(8,128)(2,1)S(1)} all-gather(bf16[1,10,272]{2,1,0:T(8,128)(2,1)S(1)} %bitcast.175), channel_id=2, replica_groups=mesh['section'=2,'replica'=4,'shard'=4] {'section','shard'}, dimensions={0}, use_global_device_ids=true | all-gather | bytes 48960 | tf_op jit(solution)/shard_map/all_gather | solution.py:298
  102.3 10.0 dynamic_update_slice.89
  114.6 9.9 dynamic_update_slice.90
  128.1 9.7 dynamic_update_slice.91
  174.0 15.2 %collective-permute-done.15 = bf16[272,1088]{1,0:T(8,128)(2,1)S(1)} collective-permute-done((bf16[272,1088]{1,0:T(8,128)(2,1)S(1)}, bf16[272,1088]{1,0:T(8,128)(2,1)S(1)}, u32[]{:S(2)}, u32[]{:S(2)}) %collective-permute-start.15) | collective-permute-done | bytes 591904 | tf_op jit(solution)/shard_map/ppermute | solution.py:209
  204.8 20.1 %mix_forward.2 = (bf16[256,320]{1,0:T(8,128)(2,1)S(1)}, bf16[256,320]{1,0:T(8,128)(2,1)S(1)}, bf16[256,320]{1,0:T(8,128)(2,1)S(1)}, bf16[256,320]{1,0:T(8,128)(2,1)S(1)}, f32[1024,128]{1,0:T(8,128)S(1)}) custom-call(s32[1]{0:T(128)} %bitcast.1.place_ref, s32[1,1024]{1,0:T(1,128)S(1)} %fusion.360.seg_row_ref, s32[1024,1]{1,0:T(8,128)S(1)} %copy.292.seg_col_ref, ...), custom_call_target="tpu_custom_call" | custom-call | flops 2684354560 | bytes 2621440 | tf_op jit(solution)/shard_map/mix_forward/pallas_call | solution.py:156
  302.6 9.7 collective-permute-done.22
  318.0 12.3 collective-permute-done.27
  330.4 10.7 collective-permute-done.25
  347.4 20.1 %mix_forward.3 = (bf16[256,320]{1,0:T(8,128)(2,1)S(1)}, bf16[256,320]{1,0:T(8,128)(2,1)S(1)}, bf16[256,320]{1,0:T(8,128)(2,1)S(1)}, bf16[256,320]{1,0:T(8,128)(2,1)S(1)}, f32[1024,128]{1,0:T(8,128)S(1)}) custom-call(s32[1]{0:T(128)} %bitcast.1.place_ref, s32[1,1024]{1,0:T(1,128)S(1)} %fusion.360.seg_row_ref, s32[1024,1]{1,0:T(8,128)S(1)} %copy.292.seg_col_ref, ...), custom_call_target="tpu_custom_call" | custom-call | flops 2684354560 | bytes 2621440 | tf_op jit(solution)/shard_map/mix_forward/pallas_call | solution.py:156
  493.4 26.8 %mix_backward.2 = (bf16[256,960]{1,0:T(8,128)(2,1)S(1)}, bf16[256,960]{1,0:T(8,128)(2,1)S(1)}, bf16[256,960]{1,0:T(8,128)(2,1)S(1)}, bf16[256,960]{1,0:T(8,128)(2,1)S(1)}) custom-call(s32[1]{0:T(128)} %bitcast.1.place_ref, s32[1,1024]{1,0:T(1,128)S(1)} %fusion.360.seg_row_ref, s32[1024,1]{1,0:T(8,128)S(1)} %copy.292.seg_col_ref, f32[1024,128]{1,0:T(8,128)S(1)} %copy-done.11, ...), custom_call_target="tpu_custom_call" | custom-call | flops 6710886400 | bytes 5242880 | tf_op jit(solution)/shard_map/mix_backward/pallas_call | solution.py:181
  651.1 26.6 %mix_backward.3 = (bf16[256,960]{1,0:T(8,128)(2,1)S(1)}, bf16[256,960]{1,0:T(8,128)(2,1)S(1)}, bf16[256,960]{1,0:T(8,128)(2,1)S(1)}, bf16[256,960]{1,0:T(8,128)(2,1)S(1)}) custom-call(s32[1]{0:T(128)} %bitcast.1.place_ref, s32[1,1024]{1,0:T(1,128)S(1)} %fusion.360.seg_row_ref, s32[1024,1]{1,0:T(8,128)S(1)} %copy.292.seg_col_ref, f32[1024,128]{1,0:T(8,128)S(1)} %copy-done.9, ...), custom_call_target="tpu_custom_call" | custom-call | flops 6710886400 | bytes 5242880 | tf_op jit(solution)/shard_map/mix_backward/pallas_call | solution.py:181
  772.7 21.7 %collective-permute-done.143 = bf16[272,1088]{1,0:T(8,128)(2,1)S(1)} collective-permute-done((bf16[272,1088]{1,0:T(8,128)(2,1)S(1)}, bf16[272,1088]{1,0:T(8,128)(2,1)S(1)}, u32[]{:S(2)}, u32[]{:S(2)}) %collective-permute-start.143) | collective-permute-done | bytes 591904 | tf_op jit(solution)/shard_map/ppermute | solution.py:209
  821.5 9.1 collective-permute-done.97
  870.6 16.5 %collective-permute-start.78 = (bf16[272,960]{1,0:T(8,128)(2,1)S(1)}, bf16[272,960]{1,0:T(8,128)(2,1)S(1)}, u32[]{:S(2)}, u32[]{:S(2)}) collective-permute-start(bf16[272,960]{1,0:T(8,128)(2,1)S(1)} %get-tuple-element.143), channel_id=1, source_target_pairs={{0,4},{12,8},{1,5},{13,9},{2,6},{14,10},{3,7},{15,11}} | collective-permute-start | bytes 1566728 | tf_op jit(solution)/shard_map/ppermute | solution.py:242
  902.7 10.7 collective-permute-done.112
  924.0 23.5 %collective-permute-done.139 = bf16[272,1088]{1,0:T(8,128)(2,1)S(1)} collective-permute-done((bf16[272,1088]{1,0:T(8,128)(2,1)S(1)}, bf16[272,1088]{1,0:T(8,128)(2,1)S(1)}, u32[]{:S(2)}, u32[]{:S(2)}) %collective-permute-start.139) | collective-permute-done | bytes 591904 | tf_op jit(solution)/shard_map/ppermute | solution.py:209
  1004.1 14.5 %collective-permute-start.156 = (bf16[1088,1088]{1,0:T(8,128)(2,1)S(1)}, bf16[1088,1088]{1,0:T(8,128)(2,1)}, u32[]{:S(2)}, u32[]{:S(2)}) collective-permute-start(bf16[1088,1088]{1,0:T(8,128)(2,1)S(1)} %copy-done.27), channel_id=1, source_target_pairs={{0,4},{12,8},{1,5},{13,9},{2,6},{14,10},{3,7},{15,11}} | collective-permute-start | bytes 7102472 | tf_op jit(solution)/shard_map/ppermute | solution.py:242
  1051.5 42.0 %collective-permute-done.134 = bf16[272,1088]{1,0:T(8,128)(2,1)S(1)} collective-permute-done((bf16[272,1088]{1,0:T(8,128)(2,1)S(1)}, bf16[272,1088]{1,0:T(8,128)(2,1)S(1)}, u32[]{:S(2)}, u32[]{:S(2)}) %collective-permute-start.134) | collective-permute-done | bytes 591904 | tf_op jit(solution)/shard_map/ppermute | solution.py:242
  1108.1 24.9 %collective-permute-done.142 = bf16[272,1088]{1,0:T(8,128)(2,1)S(1)} collective-permute-done((bf16[272,1088]{1,0:T(8,128)(2,1)S(1)}, bf16[272,1088]{1,0:T(8,128)(2,1)S(1)}, u32[]{:S(2)}, u32[]{:S(2)}) %collective-permute-start.142) | collective-permute-done | bytes 591904 | tf_op jit(solution)/shard_map/ppermute | solution.py:242
  1229.2 20.3 %dynamic_update_slice.108 = f32[272,3,1280]{2,1,0:T(4,128)} dynamic-update-slice(f32[272,3,1280]{2,1,0:T(4,128)} %broadcast_in_dim.43, f32[272,3,320]{2,1,0:T(4,128)} %copy.309, s32[]{:T(128)} %constant.83.clone.1, s32[]{:T(128)} %constant.83.clone.1, s32[]{:T(128)S(6)} %select_n.402) | dynamic-update-slice | bytes 2088964 | tf_op jit(solution)/shard_map/dynamic_update_slice | solution.py:224
  1249.5 49.5 %dynamic_update_slice.109 = f32[272,3,1280]{2,1,0:T(4,128)} dynamic-update-slice(f32[272,3,1280]{2,1,0:T(4,128)} %dynamic_update_slice.108, f32[272,3,320]{2,1,0:T(4,128)} %copy.311, s32[]{:T(128)} %constant.83.clone.1, s32[]{:T(128)} %constant.83.clone.1, s32[]{:T(128)S(6)} %select_n.404) | dynamic-update-slice | bytes 2088964 | tf_op jit(solution)/shard_map/dynamic_update_slice | solution.py:224
  1299.1 20.2 %dynamic_update_slice.110 = f32[272,3,1280]{2,1,0:T(4,128)} dynamic-update-slice(f32[272,3,1280]{2,1,0:T(4,128)} %dynamic_update_slice.109, f32[272,3,320]{2,1,0:T(4,128)} %copy.313, s32[]{:T(128)} %constant.83.clone.1, s32[]{:T(128)} %constant.83.clone.1, s32[]{:T(128)S(6)} %select_n.406) | dynamic-update-slice | bytes 2088964 | tf_op jit(solution)/shard_map/dynamic_update_slice | solution.py:224
  1319.3 48.9 %dynamic_update_slice.111 = f32[272,3,1280]{2,1,0:T(4,128)} dynamic-update-slice(f32[272,3,1280]{2,1,0:T(4,128)} %dynamic_update_slice.110, f32[272,3,320]{2,1,0:T(4,128)} %copy.315, s32[]{:T(128)} %constant.83.clone.1, s32[]{:T(128)} %constant.83.clone.1, s32[]{:T(128)S(6)} %select_n.408) | dynamic-update-slice | bytes 2088964 | tf_op jit(solution)/shard_map/dynamic_update_slice | solution.py:224
  (966 shorter events, 871.4 us)
Async XLA Ops:
  2.1 135.8 %collective-permute-start.6 = (bf16[256,1088]{0,1:T(8,128)(2,1)S(1)}, bf16[256,1088]{0,1:T(8,128)(2,1)}, u32[]{:S(2)}, u32[]{:S(2)}) collective-permute-start(bf16[256,1088]{0,1:T(8,128)(2,1)S(1)} %get-tuple-element.112), channel_id=1, source_target_pairs={{0,3},{1,2},{2,1},{3,0},{4,7},{5,6},{6,5},{7,4},{8,11},{9,10},{10,... | collective-permute-start | bytes 1671176 | tf_op jit(solution)/shard_map/ppermute | solution.py:209
  6.1 135.1 %collective-permute-start.4 = (bf16[256,1088]{0,1:T(8,128)(2,1)S(1)}, bf16[256,1088]{0,1:T(8,128)(2,1)}, u32[]{:S(2)}, u32[]{:S(2)}) collective-permute-start(bf16[256,1088]{0,1:T(8,128)(2,1)S(1)} %get-tuple-element.112), channel_id=1, source_target_pairs={{0,1},{1,0},{2,3},{3,2},{4,5},{5,4},{6,7},{7,6},{8,9},{9,8},{10,11... | collective-permute-start | bytes 1671176 | tf_op jit(solution)/shard_map/ppermute | solution.py:209
  23.0 74.4 %collective-permute-start = (bf16[272,960]{1,0:T(8,128)(2,1)}, bf16[272,960]{1,0:T(8,128)(2,1)}, u32[]{:S(2)}, u32[]{:S(2)}) collective-permute-start(bf16[272,960]{1,0:T(8,128)(2,1)} %copy.280), channel_id=1, source_target_pairs={{0,1},{1,0},{2,3},{3,2},{4,5},{5,4},{6,7},{7,6},{8,9},{9,8},{10,11... | collective-permute-start | bytes 1566728 | tf_op jit(solution)/shard_map/ppermute | solution.py:209
  28.1 84.2 %collective-permute-start.1 = (bf16[272,960]{1,0:T(8,128)(2,1)}, bf16[272,960]{1,0:T(8,128)(2,1)}, u32[]{:S(2)}, u32[]{:S(2)}) collective-permute-start(bf16[272,960]{1,0:T(8,128)(2,1)} %copy.283), channel_id=1, source_target_pairs={{0,2},{1,3},{2,0},{3,1},{4,6},{5,7},{6,4},{7,5},{8,10},{9,11},{10,... | collective-permute-start | bytes 1566728 | tf_op jit(solution)/shard_map/ppermute | solution.py:209
  30.9 93.6 %collective-permute-start.2 = (bf16[272,960]{1,0:T(8,128)(2,1)}, bf16[272,960]{1,0:T(8,128)(2,1)}, u32[]{:S(2)}, u32[]{:S(2)}) collective-permute-start(bf16[272,960]{1,0:T(8,128)(2,1)} %copy.286), channel_id=1, source_target_pairs={{0,3},{1,2},{2,1},{3,0},{4,7},{5,6},{6,5},{7,4},{8,11},{9,10},{10,... | collective-permute-start | bytes 1566728 | tf_op jit(solution)/shard_map/ppermute | solution.py:209
  169.0 86.5 %collective-permute-start.13 = (bf16[1088,1088]{1,0:T(8,128)(2,1)}, bf16[1088,1088]{1,0:T(8,128)(2,1)}, u32[]{:S(2)}, u32[]{:S(2)}) collective-permute-start(bf16[1088,1088]{1,0:T(8,128)(2,1)} %constant_dynamic-update-slice_fusion.3), channel_id=1, source_target_pairs={{0,16},{16,0},{1,17},{17,1},{2,18},{18,2},{3,19},{19,3},{4,20},{20... | collective-permute-start | bytes 7102472 | tf_op jit(solution)/shard_map/ppermute | solution.py:215
  191.0 70.7 %collective-permute-start.17 = (bf16[1088,1088]{1,0:T(8,128)(2,1)}, bf16[1088,1088]{1,0:T(8,128)(2,1)}, u32[]{:S(2)}, u32[]{:S(2)}) collective-permute-start(bf16[1088,1088]{1,0:T(8,128)(2,1)} %constant_dynamic-update-slice_fusion), channel_id=1, source_target_pairs={{0,16},{16,0},{1,17},{17,1},{2,18},{18,2},{3,19},{19,3},{4,20},{20... | collective-permute-start | bytes 7102472 | tf_op jit(solution)/shard_map/ppermute | solution.py:215
  234.0 62.1 %collective-permute-start.42 = (bf16[256,1088]{0,1:T(8,128)(2,1)}, bf16[256,1088]{0,1:T(8,128)(2,1)}, u32[]{:S(2)}, u32[]{:S(2)}) collective-permute-start(bf16[256,1088]{0,1:T(8,128)(2,1)} %get-tuple-element.90), channel_id=1, source_target_pairs={{0,3},{1,2},{2,1},{3,0},{4,7},{5,6},{6,5},{7,4},{8,11},{9,10},{10,... | collective-permute-start | bytes 1671176 | tf_op jit(solution)/shard_map/ppermute | solution.py:209
  248.8 122.2 %collective-permute-start.40 = (bf16[256,1088]{0,1:T(8,128)(2,1)}, bf16[256,1088]{0,1:T(8,128)(2,1)}, u32[]{:S(2)}, u32[]{:S(2)}) collective-permute-start(bf16[256,1088]{0,1:T(8,128)(2,1)} %get-tuple-element.90), channel_id=1, source_target_pairs={{0,2},{1,3},{2,0},{3,1},{4,6},{5,7},{6,4},{7,5},{8,10},{9,11},{10,... | collective-permute-start | bytes 1671176 | tf_op jit(solution)/shard_map/ppermute | solution.py:209
  252.7 142.6 %collective-permute-start.38 = (bf16[256,1088]{0,1:T(8,128)(2,1)}, bf16[256,1088]{0,1:T(8,128)(2,1)}, u32[]{:S(2)}, u32[]{:S(2)}) collective-permute-start(bf16[256,1088]{0,1:T(8,128)(2,1)} %get-tuple-element.90), channel_id=1, source_target_pairs={{0,1},{1,0},{2,3},{3,2},{4,5},{5,4},{6,7},{7,6},{8,9},{9,8},{10,11... | collective-permute-start | bytes 1671176 | tf_op jit(solution)/shard_map/ppermute | solution.py:209
  454.7 160.8 %collective-permute-start.127 = (bf16[1088,1088]{1,0:T(8,128)(2,1)}, bf16[1088,1088]{1,0:T(8,128)(2,1)}, u32[]{:S(2)}, u32[]{:S(2)}) collective-permute-start(bf16[1088,1088]{1,0:T(8,128)(2,1)} %convolution_convert_fusion.4), channel_id=1, source_target_pairs={{0,16},{1,17},{2,18},{3,19},{4,20},{5,21},{6,22},{7,23},{8,24},{9,... | collective-permute-start | bytes 7102472 | tf_op jit(solution)/shard_map/ppermute | solution.py:229
  457.4 161.9 %collective-permute-start.159 = (bf16[1088,1088]{1,0:T(8,128)(2,1)}, bf16[1088,1088]{1,0:T(8,128)(2,1)}, u32[]{:S(2)}, u32[]{:S(2)}) collective-permute-start(bf16[1088,1088]{1,0:T(8,128)(2,1)} %convolution_convert_fusion.2), channel_id=1, source_target_pairs={{0,16},{1,17},{2,18},{3,19},{4,20},{5,21},{6,22},{7,23},{8,24},{9,... | collective-permute-start | bytes 7102472 | tf_op jit(solution)/shard_map/ppermute | solution.py:229
  557.5 147.5 %collective-permute-start.116 = (bf16[1088,1088]{1,0:T(8,128)(2,1)}, bf16[1088,1088]{1,0:T(8,128)(2,1)}, u32[]{:S(2)}, u32[]{:S(2)}) collective-permute-start(bf16[1088,1088]{1,0:T(8,128)(2,1)} %convolution_convert_fusion), channel_id=1, source_target_pairs={{0,16},{1,17},{2,18},{3,19},{4,20},{5,21},{6,22},{7,23},{8,24},{9,... | collective-permute-start | bytes 7102472 | tf_op jit(solution)/shard_map/ppermute | solution.py:229
  591.5 104.2 %collective-permute-start.81 = (bf16[1088,960]{0,1:T(8,128)(2,1)}, bf16[1088,960]{0,1:T(8,128)(2,1)}, u32[]{:S(2)}, u32[]{:S(2)}) collective-permute-start(bf16[1088,960]{0,1:T(8,128)(2,1)} %copy.306), channel_id=1, source_target_pairs={{0,16},{1,17},{2,18},{3,19},{4,20},{5,21},{6,22},{7,23},{8,24},{9,... | collective-permute-start | bytes 6266888 | tf_op jit(solution)/shard_map/ppermute | solution.py:229
  647.6 95.2 %collective-permute-start.76 = (f32[10,272]{1,0:T(8,128)}, f32[10,272]{1,0:T(8,128)}, u32[]{:S(2)}, u32[]{:S(2)}) collective-permute-start(f32[10,272]{1,0:T(8,128)} %add.882), channel_id=1, source_target_pairs={{20,16},{24,28},{21,17},{25,29},{22,18},{26,30},{23,19},{27,31}} | collective-permute-start | bytes 32648 | tf_op jit(solution)/shard_map/ppermute | solution.py:242
  649.6 83.7 %collective-permute-start.128 = (bf16[272,1088]{1,0:T(8,128)(2,1)}, bf16[272,1088]{1,0:T(8,128)(2,1)}, u32[]{:S(2)}, u32[]{:S(2)}) collective-permute-start(bf16[272,1088]{1,0:T(8,128)(2,1)} %get-tuple-element.126), channel_id=1, source_target_pairs={{16,20},{28,24},{17,21},{29,25},{18,22},{30,26},{19,23},{31,27}} | collective-permute-start | bytes 1775624 | tf_op jit(solution)/shard_map/ppermute | solution.py:242
  760.6 84.3 %collective-permute-start.123 = (bf16[1088,1088]{1,0:T(8,128)(2,1)}, bf16[1088,1088]{1,0:T(8,128)(2,1)S(1)}, u32[]{:S(2)}, u32[]{:S(2)}) collective-permute-start(bf16[1088,1088]{1,0:T(8,128)(2,1)} %convolution_convert_fusion.5), channel_id=1, source_target_pairs={{16,0},{17,1},{18,2},{19,3},{20,4},{21,5},{22,6},{23,7},{24,8},{25... | collective-permute-start | bytes 7102472 | tf_op jit(solution)/shard_map/ppermute | solution.py:229
  913.4 106.2 %collective-permute-start.130 = (bf16[272,1088]{1,0:T(8,128)(2,1)S(1)}, bf16[272,1088]{1,0:T(8,128)(2,1)S(1)}, u32[]{:S(2)}, u32[]{:S(2)}) collective-permute-start(bf16[272,1088]{1,0:T(8,128)(2,1)S(1)} %copy-done.49), channel_id=1, source_target_pairs={{20,16},{24,28},{21,17},{25,29},{22,18},{26,30},{23,19},{27,31}} | collective-permute-start | bytes 1775624 | tf_op jit(solution)/shard_map/ppermute | solution.py:242
  974.5 123.7 %collective-permute-start.84 = (bf16[272,960]{1,0:T(8,128)(2,1)}, bf16[272,960]{1,0:T(8,128)(2,1)}, u32[]{:S(2)}, u32[]{:S(2)}) collective-permute-start(bf16[272,960]{1,0:T(8,128)(2,1)} %add_convert_fusion.46), channel_id=1, source_target_pairs={{20,16},{24,28},{21,17},{25,29},{22,18},{26,30},{23,19},{27,31}} | collective-permute-start | bytes 1566728 | tf_op jit(solution)/shard_map/ppermute | solution.py:242
  987.2 63.5 %collective-permute-start.138 = (bf16[272,1088]{1,0:T(8,128)(2,1)}, bf16[272,1088]{1,0:T(8,128)(2,1)}, u32[]{:S(2)}, u32[]{:S(2)}) collective-permute-start(bf16[272,1088]{1,0:T(8,128)(2,1)} %add_convert_fusion.20), channel_id=1, source_target_pairs={{20,16},{24,28},{21,17},{25,29},{22,18},{26,30},{23,19},{27,31}} | collective-permute-start | bytes 1775624 | tf_op jit(solution)/shard_map/ppermute | solution.py:242
  1105.9 277.0 %collective-permute-start.162 = (bf16[1088,1088]{1,0:T(8,128)(2,1)S(1)}, bf16[1088,1088]{1,0:T(8,128)(2,1)}, u32[]{:S(2)}, u32[]{:S(2)}) collective-permute-start(bf16[1088,1088]{1,0:T(8,128)(2,1)S(1)} %add_convert_fusion), channel_id=1, source_target_pairs={{20,16},{24,28},{21,17},{25,29},{22,18},{26,30},{23,19},{27,31}} | collective-permute-start | bytes 7102472 | tf_op jit(solution)/shard_map/ppermute | solution.py:242
  1133.0 249.9 %collective-permute-start.158 = (bf16[1088,1088]{1,0:T(8,128)(2,1)}, bf16[1088,1088]{1,0:T(8,128)(2,1)}, u32[]{:S(2)}, u32[]{:S(2)}) collective-permute-start(bf16[1088,1088]{1,0:T(8,128)(2,1)} %add_convert_fusion.3), channel_id=1, source_target_pairs={{4,0},{8,12},{5,1},{9,13},{6,2},{10,14},{7,3},{11,15}} | collective-permute-start | bytes 7102472 | tf_op jit(solution)/shard_map/ppermute | solution.py:242
  1185.1 195.2 %collective-permute-start.122 = (bf16[272,1088]{1,0:T(8,128)(2,1)S(1)}, bf16[272,1088]{1,0:T(8,128)(2,1)}, u32[]{:S(2)}, u32[]{:S(2)}) collective-permute-start(bf16[272,1088]{1,0:T(8,128)(2,1)S(1)} %add_convert_fusion.28), channel_id=1, source_target_pairs={{20,16},{24,28},{21,17},{25,29},{22,18},{26,30},{23,19},{27,31}} | collective-permute-start | bytes 1775624 | tf_op jit(solution)/shard_map/ppermute | solution.py:242
  1191.1 189.2 %collective-permute-start.115 = (bf16[272,1088]{1,0:T(8,128)(2,1)}, bf16[272,1088]{1,0:T(8,128)(2,1)}, u32[]{:S(2)}, u32[]{:S(2)}) collective-permute-start(bf16[272,1088]{1,0:T(8,128)(2,1)} %add_convert_fusion.31), channel_id=1, source_target_pairs={{4,0},{8,12},{5,1},{9,13},{6,2},{10,14},{7,3},{11,15}} | collective-permute-start | bytes 1775624 | tf_op jit(solution)/shard_map/ppermute | solution.py:242
  (316 other events, 5257.0 us)
